TPU v7x, 128 devices: a whole 4x4x4 slice. The times are simulated.
128 devices in a mesh: depth: 8 (over z, core), rows: 16 (over y, x).
Axes of the slice: x: 4, y: 4, z: 4, core: 2. Of those that a mesh axis runs over, the one named last changes fastest.
Arguments:
- density: float32 [128, 2048, 2048], P('depth', 'rows'), may hold values from 0.2 to 3
- occupancy: int32 [8, 16, 16], P('depth', 'rows'), may hold values from 0 to 1, as said below
- transfer: float32 [2, 4], replicated, may hold values from -1.5 to 1.5
Outputs:
- image: float32 [4, 2048, 2048], P(None, 'rows', 'depth')
Inputs may be any that keep to these rules, and one draw needn't show every extreme that they name: `occupancy`: each entry is 0 or 1 and flags a block of 16 x 128 x 128 cells as occupied; at most 12 of the blocks of one device's brick are occupied, and some brick has exactly 12.
All inputs are finite; a program needn't handle non-finite values.
Results may differ from a plain program's by a relative error of at most 0.000079.
Values sent between devices are 32-bit elements; how exact they have to be, the bound alone decides.
A program may use at most 256 MiB of HBM per device.

v0:
```python
import jax
import jax.numpy as jnp
from jax import lax
from jax.sharding import PartitionSpec as P


def with_halo(x, sides, width):
    edges = {}
    for axis, dim in sides:
        size, length = (lax.axis_size(axis), x.shape[dim])
        up = [(i, (i + 1) % size) for i in range(size - 1)]
        last = lax.slice_in_dim(x, length - width, length, axis=dim)
        leading = lax.slice_in_dim(x, 0, width, axis=dim)
        edges[dim] = (
            lax.ppermute(last, axis, up),
            lax.ppermute(leading, axis, [(b, a) for a, b in up]),
        )
    done = []
    for _, dim in sides:
        low, high = edges[dim]
        around = [(width, width) if d in done else (0, 0) for d in range(x.ndim)]
        x = jnp.concatenate([jnp.pad(low, around), x, jnp.pad(high, around)], axis=dim)
        done.append(dim)
    return x


def swapped(block, axis, bit):
    count = lax.axis_size(axis)
    route = []
    for low in range(count):
        high = low | 1 << bit
        if high != low and high < count:
            route += [(low, high), (high, low)]
    return lax.ppermute(block, axis, route)


def shade(center, grad_z, grad_y, grad_x, transfer, ray_step):
    inv_norm = 1.0 / jnp.sqrt(grad_x * grad_x + grad_y * grad_y + grad_z * grad_z + 1.0)
    lighting = 0.3 + 0.7 * jnp.abs((0.48 * grad_z + 0.6 * grad_y + 0.64 * grad_x) * inv_norm)
    extinct = center * jax.nn.softplus(transfer[0, 3] * center + transfer[1, 3])
    opacity = 1.0 - jnp.exp(-ray_step * extinct)
    colors = jnp.stack(
        [
            jax.nn.sigmoid(transfer[0, channel] * center + transfer[1, channel])
            for channel in range(3)
        ]
    )
    return (opacity * lighting * colors, opacity)


def voxels(window, transfer, ray_step):
    center = window[1, 1:-1, ..., 1:-1]
    grad_z = (window[2, 1:-1, ..., 1:-1] - window[0, 1:-1, ..., 1:-1]) * 0.5
    grad_y = (window[1, 2:, ..., 1:-1] - window[1, :-2, ..., 1:-1]) * 0.5
    grad_x = (window[1, 1:-1, ..., 2:] - window[1, 1:-1, ..., :-2]) * 0.5
    return shade(center, grad_z, grad_y, grad_x, transfer, ray_step)


def march(padded, transfer, ray_step):
    depth_count = padded.shape[0] - 2
    cell_shape = (padded.shape[1] - 2,) + padded.shape[2:-1] + (padded.shape[-1] - 2,)
    start_state = (jnp.zeros((3,) + cell_shape, jnp.float32), jnp.ones(cell_shape, jnp.float32))

    def advance(state_pair, depth_at):
        color_sum, transmit = state_pair
        window = lax.dynamic_slice_in_dim(padded, depth_at, 3, 0)
        shaded, opacity = voxels(window, transfer, ray_step)
        return ((color_sum + transmit * shaded, transmit * (1.0 - opacity)), None)

    (color_sum, transmit), _ = lax.scan(
        advance, start_state, jnp.arange(depth_count, dtype=jnp.int32)
    )
    return (color_sum, transmit)


def blend_over(front_part, back_part):
    color_sum = front_part[:3] + front_part[3:] * back_part[:3]
    transmit = front_part[3:] * back_part[3:]
    return jnp.concatenate([color_sum, transmit], 0)


def shards(density, occupancy, transfer):
    depth_cells, row_cells, col_cells = density.shape
    block_flags = occupancy.reshape(-1)
    block_count = block_flags.shape[0]
    block_width = col_cells // block_count
    depth_devices = lax.axis_size("depth")
    position = lax.axis_index("depth")
    masked = (
        density.reshape(depth_cells, row_cells, block_count, block_width)
        * block_flags.astype(jnp.float32)[None, None, :, None]
    )
    masked = masked.reshape(depth_cells, row_cells, col_cells)
    extended = with_halo(masked, (("depth", 0), ("rows", 1)), 1)
    ray_step = 2.0 / (depth_cells * depth_devices)
    padded = jnp.pad(extended, ((0, 0), (0, 0), (1, 1)))
    color_sum, transmit = march(padded, transfer, ray_step)
    layers = jnp.concatenate([color_sum, transmit[None]], 0)
    piece_width = col_cells // depth_devices
    levels = depth_devices.bit_length() - 1
    merged = layers.reshape((4, row_cells) + (2,) * levels + (piece_width,))
    for bit_level in range(levels):
        axis_at = 2 + levels - 1 - bit_level
        own_bit = position >> bit_level & 1
        kept_half = lax.dynamic_index_in_dim(merged, own_bit, axis_at, keepdims=False)
        sent_half = lax.dynamic_index_in_dim(merged, 1 - own_bit, axis_at, keepdims=False)
        partner_half = swapped(sent_half, "depth", bit_level)
        front_half = jnp.where(own_bit == 0, kept_half, partner_half)
        back_half = jnp.where(own_bit == 0, partner_half, kept_half)
        merged = blend_over(front_half, back_half)
    return jnp.concatenate([merged[:3], 1.0 - merged[3:]], 0)


def solution(mesh):
    in_specs = (P("depth", "rows", None), P("depth", "rows", None), P())
    out_specs = P(None, "rows", "depth")
    return jax.shard_map(shards, mesh=mesh, in_specs=in_specs, out_specs=out_specs, check_vma=False)
```

profile of v0, /device:TPU:24, one launch (start us, length us, event | category | flops | bytes accessed | tf_op | source)
XLA Modules:
  0.0 509.5 jit_solution(5697674330012559538)
XLA Ops:
  0.7 9.4 %copy.8 = f32[256,8,16,128]{3,2,1,0:T(8,128)S(1)} copy(f32[256,8,16,128]{3,1,2,0:T(8,128)} %bitcast.98) | data formatting | bytes 33554432
  18.7 7.4 %broadcast_multiply_fusion = f32[16,128,2048]{2,1,0:T(8,128)S(1)} fusion(f32[16,128,2048]{2,1,0:T(8,128)} %param.5, f32[2048]{0:T(1024)S(1)} %broadcast_bitcast_fusion), kind=kLoop, calls=%fused_computation.37 | loop fusion | flops 4194304 | bytes 33562624 | tf_op jit(solution)/shard_map/mul | solution.py:90
  26.2 5.7 %copy-done.4 = f32[16,128,2048]{2,1,0:T(8,128)} copy-done((f32[16,128,2048]{2,1,0:T(8,128)}, f32[16,128,2048]{2,1,0:T(8,128)S(1)}, u32[]{:S(2)}) %copy-start.4) | copy-done | bytes 16777240
  44.0 10.1 %select_maximum_fusion = f32[18,130,2048]{2,1,0:T(8,128)S(1)} fusion(f32[16,1,2048]{2,1,0:T(1,128)S(1)} %collective-permute-done.3, f32[16,1,2048]{2,1,0:T(1,128)S(1)} %collective-permute-done, f32[1,128,2048]{2,1,0:T(8,128)} %collective-permute-done.2, f32[16,128,2048]{2,1,0:T(8,128)} %copy-done.4, f32[1,128,2048]{2,1,0:T(8,128)} %collective-permute-done.1), kind=kLoop, calls=%fused_computation.32 | loop fusion | flops 38338560 | bytes 38305792 | tf_op jit(solution)/shard_map/concatenate | solution.py:22
  54.2 9.5 %pad.13 = f32[18,130,2050]{2,1,0:T(8,128)} pad(f32[18,130,2048]{2,1,0:T(8,128)S(1)} %select_maximum_fusion, f32[]{:T(128)} %constant.103.clone.1), padding=0_0x0_0x1_1 | pad | bytes 38357284 | tf_op jit(solution)/shard_map/jit(_pad)/pad | solution.py:96
  63.7 383.4 %while.15 = (s32[]{:T(128)}, f32[3,128,2048]{2,1,0:T(8,128)S(1)}, f32[128,2048]{1,0:T(8,128)}, s32[16]{0:T(128)S(1)}, f32[18,130,2050]{2,1,0:T(8,128)}, /*index=...) while((s32[]{:T(128)}, f32[3,128,2048]{2,1,0:T(8,128)S(1)}, ...), condition=%wide.region_1.2_spmd.clone, body=%wide.region_0.1_spmd.clone.sunk | while | flops 20971528 | bytes 44040648 | solution.py:70
  66.9 13.4 %fusion.43 = (f32[128,2048]{1,0:T(8,128)}, f32[1,128,2048]{2,1,0:T(8,128)}, f32[1,128,2048]{2,1,0:T(8,128)}, f32[1,128,2048]{2,1,0:T(8,128)}) fusion(f32[18,130,2050]{2,1,0:T(8,128)} %get-tuple-element.243, s32[]{:T(128)S(6)} %add.313, s32[]{:T(128)S(6)} %add.314, s32[]{:T(128)S(6)} %add.315, s32[]{:T(128)S(6)} %select_n.137, s32[]{:T(128)S(6)} %add.316, ...), kind=kLoop, calls=%fused_computation.10.clone.1 | loop fusion | flops 12582912 | bytes 11534388 | tf_op jit(solution)/shard_map/while/body/eval_jaxpr/mul | solution.py:48
  90.3 13.5 %fusion.43 = (f32[128,2048]{1,0:T(8,128)}, f32[1,128,2048]{2,1,0:T(8,128)}, f32[1,128,2048]{2,1,0:T(8,128)}, f32[1,128,2048]{2,1,0:T(8,128)}) fusion(f32[18,130,2050]{2,1,0:T(8,128)} %get-tuple-element.243, s32[]{:T(128)S(6)} %add.313, s32[]{:T(128)S(6)} %add.314, s32[]{:T(128)S(6)} %add.315, s32[]{:T(128)S(6)} %select_n.137, s32[]{:T(128)S(6)} %add.316, ...), kind=kLoop, calls=%fused_computation.10.clone.1 | loop fusion | flops 12582912 | bytes 11534388 | tf_op jit(solution)/shard_map/while/body/eval_jaxpr/mul | solution.py:48
  103.8 5.4 %fusion.44 = (f32[128,2048]{1,0:T(8,128)}, f32[128,2048]{1,0:T(8,128)S(1)}) fusion(f32[18,130,2050]{2,1,0:T(8,128)} %get-tuple-element.243, s32[]{:T(128)S(6)} %add.313, s32[]{:T(128)S(6)} %add.314, f32[]{:T(128)} %bitcast.90, f32[]{:T(128)} %bitcast.91, f32[128,2048]{1,0:T(8,128)} %get-tuple-element.230, pred[]{:T(512)S(6)} %compare.14), kind=kLoop, calls=%fused_computation.16.clone.1 | loop fusion | flops 3670016 | bytes 4194321 | tf_op jit(solution)/shard_map/while/body/eval_jaxpr/mul | solution.py:68
  114.1 13.7 %fusion.43 = (f32[128,2048]{1,0:T(8,128)}, f32[1,128,2048]{2,1,0:T(8,128)}, f32[1,128,2048]{2,1,0:T(8,128)}, f32[1,128,2048]{2,1,0:T(8,128)}) fusion(f32[18,130,2050]{2,1,0:T(8,128)} %get-tuple-element.243, s32[]{:T(128)S(6)} %add.313, s32[]{:T(128)S(6)} %add.314, s32[]{:T(128)S(6)} %add.315, s32[]{:T(128)S(6)} %select_n.137, s32[]{:T(128)S(6)} %add.316, ...), kind=kLoop, calls=%fused_computation.10.clone.1 | loop fusion | flops 12582912 | bytes 11534388 | tf_op jit(solution)/shard_map/while/body/eval_jaxpr/mul | solution.py:48
  127.9 5.4 %fusion.44 = (f32[128,2048]{1,0:T(8,128)}, f32[128,2048]{1,0:T(8,128)S(1)}) fusion(f32[18,130,2050]{2,1,0:T(8,128)} %get-tuple-element.243, s32[]{:T(128)S(6)} %add.313, s32[]{:T(128)S(6)} %add.314, f32[]{:T(128)} %bitcast.90, f32[]{:T(128)} %bitcast.91, f32[128,2048]{1,0:T(8,128)} %get-tuple-element.230, pred[]{:T(512)S(6)} %compare.14), kind=kLoop, calls=%fused_computation.16.clone.1 | loop fusion | flops 3670016 | bytes 4194321 | tf_op jit(solution)/shard_map/while/body/eval_jaxpr/mul | solution.py:68
  138.2 13.6 %fusion.43 = (f32[128,2048]{1,0:T(8,128)}, f32[1,128,2048]{2,1,0:T(8,128)}, f32[1,128,2048]{2,1,0:T(8,128)}, f32[1,128,2048]{2,1,0:T(8,128)}) fusion(f32[18,130,2050]{2,1,0:T(8,128)} %get-tuple-element.243, s32[]{:T(128)S(6)} %add.313, s32[]{:T(128)S(6)} %add.314, s32[]{:T(128)S(6)} %add.315, s32[]{:T(128)S(6)} %select_n.137, s32[]{:T(128)S(6)} %add.316, ...), kind=kLoop, calls=%fused_computation.10.clone.1 | loop fusion | flops 12582912 | bytes 11534388 | tf_op jit(solution)/shard_map/while/body/eval_jaxpr/mul | solution.py:48
  151.8 5.4 %fusion.44 = (f32[128,2048]{1,0:T(8,128)}, f32[128,2048]{1,0:T(8,128)S(1)}) fusion(f32[18,130,2050]{2,1,0:T(8,128)} %get-tuple-element.243, s32[]{:T(128)S(6)} %add.313, s32[]{:T(128)S(6)} %add.314, f32[]{:T(128)} %bitcast.90, f32[]{:T(128)} %bitcast.91, f32[128,2048]{1,0:T(8,128)} %get-tuple-element.230, pred[]{:T(512)S(6)} %compare.14), kind=kLoop, calls=%fused_computation.16.clone.1 | loop fusion | flops 3670016 | bytes 4194321 | tf_op jit(solution)/shard_map/while/body/eval_jaxpr/mul | solution.py:68
  162.1 13.6 %fusion.43 = (f32[128,2048]{1,0:T(8,128)}, f32[1,128,2048]{2,1,0:T(8,128)}, f32[1,128,2048]{2,1,0:T(8,128)}, f32[1,128,2048]{2,1,0:T(8,128)}) fusion(f32[18,130,2050]{2,1,0:T(8,128)} %get-tuple-element.243, s32[]{:T(128)S(6)} %add.313, s32[]{:T(128)S(6)} %add.314, s32[]{:T(128)S(6)} %add.315, s32[]{:T(128)S(6)} %select_n.137, s32[]{:T(128)S(6)} %add.316, ...), kind=kLoop, calls=%fused_computation.10.clone.1 | loop fusion | flops 12582912 | bytes 11534388 | tf_op jit(solution)/shard_map/while/body/eval_jaxpr/mul | solution.py:48
  175.7 5.4 %fusion.44 = (f32[128,2048]{1,0:T(8,128)}, f32[128,2048]{1,0:T(8,128)S(1)}) fusion(f32[18,130,2050]{2,1,0:T(8,128)} %get-tuple-element.243, s32[]{:T(128)S(6)} %add.313, s32[]{:T(128)S(6)} %add.314, f32[]{:T(128)} %bitcast.90, f32[]{:T(128)} %bitcast.91, f32[128,2048]{1,0:T(8,128)} %get-tuple-element.230, pred[]{:T(512)S(6)} %compare.14), kind=kLoop, calls=%fused_computation.16.clone.1 | loop fusion | flops 3670016 | bytes 4194321 | tf_op jit(solution)/shard_map/while/body/eval_jaxpr/mul | solution.py:68
  186.0 13.8 %fusion.43 = (f32[128,2048]{1,0:T(8,128)}, f32[1,128,2048]{2,1,0:T(8,128)}, f32[1,128,2048]{2,1,0:T(8,128)}, f32[1,128,2048]{2,1,0:T(8,128)}) fusion(f32[18,130,2050]{2,1,0:T(8,128)} %get-tuple-element.243, s32[]{:T(128)S(6)} %add.313, s32[]{:T(128)S(6)} %add.314, s32[]{:T(128)S(6)} %add.315, s32[]{:T(128)S(6)} %select_n.137, s32[]{:T(128)S(6)} %add.316, ...), kind=kLoop, calls=%fused_computation.10.clone.1 | loop fusion | flops 12582912 | bytes 11534388 | tf_op jit(solution)/shard_map/while/body/eval_jaxpr/mul | solution.py:48
  199.8 5.4 %fusion.44 = (f32[128,2048]{1,0:T(8,128)}, f32[128,2048]{1,0:T(8,128)S(1)}) fusion(f32[18,130,2050]{2,1,0:T(8,128)} %get-tuple-element.243, s32[]{:T(128)S(6)} %add.313, s32[]{:T(128)S(6)} %add.314, f32[]{:T(128)} %bitcast.90, f32[]{:T(128)} %bitcast.91, f32[128,2048]{1,0:T(8,128)} %get-tuple-element.230, pred[]{:T(512)S(6)} %compare.14), kind=kLoop, calls=%fused_computation.16.clone.1 | loop fusion | flops 3670016 | bytes 4194321 | tf_op jit(solution)/shard_map/while/body/eval_jaxpr/mul | solution.py:68
  210.1 13.9 %fusion.43 = (f32[128,2048]{1,0:T(8,128)}, f32[1,128,2048]{2,1,0:T(8,128)}, f32[1,128,2048]{2,1,0:T(8,128)}, f32[1,128,2048]{2,1,0:T(8,128)}) fusion(f32[18,130,2050]{2,1,0:T(8,128)} %get-tuple-element.243, s32[]{:T(128)S(6)} %add.313, s32[]{:T(128)S(6)} %add.314, s32[]{:T(128)S(6)} %add.315, s32[]{:T(128)S(6)} %select_n.137, s32[]{:T(128)S(6)} %add.316, ...), kind=kLoop, calls=%fused_computation.10.clone.1 | loop fusion | flops 12582912 | bytes 11534388 | tf_op jit(solution)/shard_map/while/body/eval_jaxpr/mul | solution.py:48
  224.1 5.4 %fusion.44 = (f32[128,2048]{1,0:T(8,128)}, f32[128,2048]{1,0:T(8,128)S(1)}) fusion(f32[18,130,2050]{2,1,0:T(8,128)} %get-tuple-element.243, s32[]{:T(128)S(6)} %add.313, s32[]{:T(128)S(6)} %add.314, f32[]{:T(128)} %bitcast.90, f32[]{:T(128)} %bitcast.91, f32[128,2048]{1,0:T(8,128)} %get-tuple-element.230, pred[]{:T(512)S(6)} %compare.14), kind=kLoop, calls=%fused_computation.16.clone.1 | loop fusion | flops 3670016 | bytes 4194321 | tf_op jit(solution)/shard_map/while/body/eval_jaxpr/mul | solution.py:68
  234.4 13.8 %fusion.43 = (f32[128,2048]{1,0:T(8,128)}, f32[1,128,2048]{2,1,0:T(8,128)}, f32[1,128,2048]{2,1,0:T(8,128)}, f32[1,128,2048]{2,1,0:T(8,128)}) fusion(f32[18,130,2050]{2,1,0:T(8,128)} %get-tuple-element.243, s32[]{:T(128)S(6)} %add.313, s32[]{:T(128)S(6)} %add.314, s32[]{:T(128)S(6)} %add.315, s32[]{:T(128)S(6)} %select_n.137, s32[]{:T(128)S(6)} %add.316, ...), kind=kLoop, calls=%fused_computation.10.clone.1 | loop fusion | flops 12582912 | bytes 11534388 | tf_op jit(solution)/shard_map/while/body/eval_jaxpr/mul | solution.py:48
  258.5 13.5 %fusion.43 = (f32[128,2048]{1,0:T(8,128)}, f32[1,128,2048]{2,1,0:T(8,128)}, f32[1,128,2048]{2,1,0:T(8,128)}, f32[1,128,2048]{2,1,0:T(8,128)}) fusion(f32[18,130,2050]{2,1,0:T(8,128)} %get-tuple-element.243, s32[]{:T(128)S(6)} %add.313, s32[]{:T(128)S(6)} %add.314, s32[]{:T(128)S(6)} %add.315, s32[]{:T(128)S(6)} %select_n.137, s32[]{:T(128)S(6)} %add.316, ...), kind=kLoop, calls=%fused_computation.10.clone.1 | loop fusion | flops 12582912 | bytes 11534388 | tf_op jit(solution)/shard_map/while/body/eval_jaxpr/mul | solution.py:48
  282.3 13.9 %fusion.43 = (f32[128,2048]{1,0:T(8,128)}, f32[1,128,2048]{2,1,0:T(8,128)}, f32[1,128,2048]{2,1,0:T(8,128)}, f32[1,128,2048]{2,1,0:T(8,128)}) fusion(f32[18,130,2050]{2,1,0:T(8,128)} %get-tuple-element.243, s32[]{:T(128)S(6)} %add.313, s32[]{:T(128)S(6)} %add.314, s32[]{:T(128)S(6)} %add.315, s32[]{:T(128)S(6)} %select_n.137, s32[]{:T(128)S(6)} %add.316, ...), kind=kLoop, calls=%fused_computation.10.clone.1 | loop fusion | flops 12582912 | bytes 11534388 | tf_op jit(solution)/shard_map/while/body/eval_jaxpr/mul | solution.py:48
  306.6 13.8 %fusion.43 = (f32[128,2048]{1,0:T(8,128)}, f32[1,128,2048]{2,1,0:T(8,128)}, f32[1,128,2048]{2,1,0:T(8,128)}, f32[1,128,2048]{2,1,0:T(8,128)}) fusion(f32[18,130,2050]{2,1,0:T(8,128)} %get-tuple-element.243, s32[]{:T(128)S(6)} %add.313, s32[]{:T(128)S(6)} %add.314, s32[]{:T(128)S(6)} %add.315, s32[]{:T(128)S(6)} %select_n.137, s32[]{:T(128)S(6)} %add.316, ...), kind=kLoop, calls=%fused_computation.10.clone.1 | loop fusion | flops 12582912 | bytes 11534388 | tf_op jit(solution)/shard_map/while/body/eval_jaxpr/mul | solution.py:48
  330.7 13.5 %fusion.43 = (f32[128,2048]{1,0:T(8,128)}, f32[1,128,2048]{2,1,0:T(8,128)}, f32[1,128,2048]{2,1,0:T(8,128)}, f32[1,128,2048]{2,1,0:T(8,128)}) fusion(f32[18,130,2050]{2,1,0:T(8,128)} %get-tuple-element.243, s32[]{:T(128)S(6)} %add.313, s32[]{:T(128)S(6)} %add.314, s32[]{:T(128)S(6)} %add.315, s32[]{:T(128)S(6)} %select_n.137, s32[]{:T(128)S(6)} %add.316, ...), kind=kLoop, calls=%fused_computation.10.clone.1 | loop fusion | flops 12582912 | bytes 11534388 | tf_op jit(solution)/shard_map/while/body/eval_jaxpr/mul | solution.py:48
  344.3 5.4 %fusion.44 = (f32[128,2048]{1,0:T(8,128)}, f32[128,2048]{1,0:T(8,128)S(1)}) fusion(f32[18,130,2050]{2,1,0:T(8,128)} %get-tuple-element.243, s32[]{:T(128)S(6)} %add.313, s32[]{:T(128)S(6)} %add.314, f32[]{:T(128)} %bitcast.90, f32[]{:T(128)} %bitcast.91, f32[128,2048]{1,0:T(8,128)} %get-tuple-element.230, pred[]{:T(512)S(6)} %compare.14), kind=kLoop, calls=%fused_computation.16.clone.1 | loop fusion | flops 3670016 | bytes 4194321 | tf_op jit(solution)/shard_map/while/body/eval_jaxpr/mul | solution.py:68
  354.6 13.5 %fusion.43 = (f32[128,2048]{1,0:T(8,128)}, f32[1,128,2048]{2,1,0:T(8,128)}, f32[1,128,2048]{2,1,0:T(8,128)}, f32[1,128,2048]{2,1,0:T(8,128)}) fusion(f32[18,130,2050]{2,1,0:T(8,128)} %get-tuple-element.243, s32[]{:T(128)S(6)} %add.313, s32[]{:T(128)S(6)} %add.314, s32[]{:T(128)S(6)} %add.315, s32[]{:T(128)S(6)} %select_n.137, s32[]{:T(128)S(6)} %add.316, ...), kind=kLoop, calls=%fused_computation.10.clone.1 | loop fusion | flops 12582912 | bytes 11534388 | tf_op jit(solution)/shard_map/while/body/eval_jaxpr/mul | solution.py:48
  378.4 13.6 %fusion.43 = (f32[128,2048]{1,0:T(8,128)}, f32[1,128,2048]{2,1,0:T(8,128)}, f32[1,128,2048]{2,1,0:T(8,128)}, f32[1,128,2048]{2,1,0:T(8,128)}) fusion(f32[18,130,2050]{2,1,0:T(8,128)} %get-tuple-element.243, s32[]{:T(128)S(6)} %add.313, s32[]{:T(128)S(6)} %add.314, s32[]{:T(128)S(6)} %add.315, s32[]{:T(128)S(6)} %select_n.137, s32[]{:T(128)S(6)} %add.316, ...), kind=kLoop, calls=%fused_computation.10.clone.1 | loop fusion | flops 12582912 | bytes 11534388 | tf_op jit(solution)/shard_map/while/body/eval_jaxpr/mul | solution.py:48
  392.1 5.4 %fusion.44 = (f32[128,2048]{1,0:T(8,128)}, f32[128,2048]{1,0:T(8,128)S(1)}) fusion(f32[18,130,2050]{2,1,0:T(8,128)} %get-tuple-element.243, s32[]{:T(128)S(6)} %add.313, s32[]{:T(128)S(6)} %add.314, f32[]{:T(128)} %bitcast.90, f32[]{:T(128)} %bitcast.91, f32[128,2048]{1,0:T(8,128)} %get-tuple-element.230, pred[]{:T(512)S(6)} %compare.14), kind=kLoop, calls=%fused_computation.16.clone.1 | loop fusion | flops 3670016 | bytes 4194321 | tf_op jit(solution)/shard_map/while/body/eval_jaxpr/mul | solution.py:68
  402.4 13.6 %fusion.43 = (f32[128,2048]{1,0:T(8,128)}, f32[1,128,2048]{2,1,0:T(8,128)}, f32[1,128,2048]{2,1,0:T(8,128)}, f32[1,128,2048]{2,1,0:T(8,128)}) fusion(f32[18,130,2050]{2,1,0:T(8,128)} %get-tuple-element.243, s32[]{:T(128)S(6)} %add.313, s32[]{:T(128)S(6)} %add.314, s32[]{:T(128)S(6)} %add.315, s32[]{:T(128)S(6)} %select_n.137, s32[]{:T(128)S(6)} %add.316, ...), kind=kLoop, calls=%fused_computation.10.clone.1 | loop fusion | flops 12582912 | bytes 11534388 | tf_op jit(solution)/shard_map/while/body/eval_jaxpr/mul | solution.py:48
  426.4 13.6 %fusion.43 = (f32[128,2048]{1,0:T(8,128)}, f32[1,128,2048]{2,1,0:T(8,128)}, f32[1,128,2048]{2,1,0:T(8,128)}, f32[1,128,2048]{2,1,0:T(8,128)}) fusion(f32[18,130,2050]{2,1,0:T(8,128)} %get-tuple-element.243, s32[]{:T(128)S(6)} %add.313, s32[]{:T(128)S(6)} %add.314, s32[]{:T(128)S(6)} %add.315, s32[]{:T(128)S(6)} %select_n.137, s32[]{:T(128)S(6)} %add.316, ...), kind=kLoop, calls=%fused_computation.10.clone.1 | loop fusion | flops 12582912 | bytes 11534388 | tf_op jit(solution)/shard_map/while/body/eval_jaxpr/mul | solution.py:48
  468.2 23.6 %collective-permute-done.5 = f32[4,128,2,256]{3,1,2,0:T(8,128)} collective-permute-done((f32[4,128,2,256]{3,1,2,0:T(8,128)S(1)}, f32[4,128,2,256]{3,1,2,0:T(8,128)}, u32[]{:S(2)}, u32[]{:S(2)}) %collective-permute-start.5) | collective-permute-done | bytes 1048608 | tf_op jit(solution)/shard_map/ppermute | solution.py:34
  496.9 11.6 %collective-permute-done.6 = f32[4,128,256]{2,1,0:T(8,128)S(1)} collective-permute-done((f32[4,128,256]{2,1,0:T(8,128)S(1)}, f32[4,128,256]{2,1,0:T(8,128)S(1)}, u32[]{:S(2)}, u32[]{:S(2)}) %collective-permute-start.6) | collective-permute-done | bytes 524320 | tf_op jit(solution)/shard_map/ppermute | solution.py:34
  (226 shorter events, 138.0 us)
Async XLA Ops:
  13.5 30.5 %collective-permute-start.1 = (f32[1,128,2048]{2,1,0:T(8,128)}, f32[1,128,2048]{2,1,0:T(8,128)}, u32[]{:S(2)}, u32[]{:S(2)}) collective-permute-start(f32[1,128,2048]{2,1,0:T(8,128)} %slice.149), channel_id=1, source_target_pairs={{0,16},{16,32},{32,48},{48,64},{64,80},{80,96},{96,112},{1,17},{17... | collective-permute-start | bytes 3145736 | tf_op jit(solution)/shard_map/ppermute | solution.py:15
  17.4 26.7 %collective-permute-start.2 = (f32[1,128,2048]{2,1,0:T(8,128)}, f32[1,128,2048]{2,1,0:T(8,128)}, u32[]{:S(2)}, u32[]{:S(2)}) collective-permute-start(f32[1,128,2048]{2,1,0:T(8,128)} %slice.151), channel_id=1, source_target_pairs={{16,0},{32,16},{48,32},{64,48},{80,64},{96,80},{112,96},{17,1},{33... | collective-permute-start | bytes 3145736 | tf_op jit(solution)/shard_map/ppermute | solution.py:16
  26.1 5.7 %copy-start.4 = (f32[16,128,2048]{2,1,0:T(8,128)}, f32[16,128,2048]{2,1,0:T(8,128)S(1)}, u32[]{:S(2)}) copy-start(f32[16,128,2048]{2,1,0:T(8,128)S(1)} %broadcast_multiply_fusion) | copy-start | bytes 50331652
  32.7 9.7 %collective-permute-start = (f32[16,1,2048]{2,1,0:T(1,128)}, f32[16,1,2048]{2,1,0:T(1,128)S(1)}, u32[]{:S(2)}, u32[]{:S(2)}) collective-permute-start(f32[16,1,2048]{2,1,0:T(1,128)} %get-tuple-element.136), channel_id=1, source_target_pairs={{0,1},{1,2},{2,3},{3,4},{4,5},{5,6},{6,7},{7,8},{8,9},{9,10},{10,1... | collective-permute-start | bytes 393224 | tf_op jit(solution)/shard_map/ppermute | solution.py:15
  36.1 7.9 %collective-permute-start.3 = (f32[16,1,2048]{2,1,0:T(1,128)S(1)}, f32[16,1,2048]{2,1,0:T(1,128)S(1)}, u32[]{:S(2)}, u32[]{:S(2)}) collective-permute-start(f32[16,1,2048]{2,1,0:T(1,128)S(1)} %get-tuple-element.137), channel_id=1, source_target_pairs={{1,0},{2,1},{3,2},{4,3},{5,4},{6,5},{7,6},{8,7},{9,8},{10,9},{11,1... | collective-permute-start | bytes 393224 | tf_op jit(solution)/shard_map/ppermute | solution.py:16
  54.2 9.5 %copy-start.5 = (f32[2,4]{1,0:T(2,128)S(1)}, f32[2,4]{1,0:T(2,128)}, u32[]{:S(2)}) copy-start(f32[2,4]{1,0:T(2,128)} %param.7) | copy-start | bytes 100
  103.8 5.5 %copy-start = (f32[128,2048]{1,0:T(8,128)S(1)}, f32[128,2048]{1,0:T(8,128)}, u32[]{:S(2)}) copy-start(f32[128,2048]{1,0:T(8,128)} %get-tuple-element.214) | copy-start | bytes 3145732 | tf_op jit(solution)/shard_map/while
  103.8 5.5 %copy-start.1 = (f32[1,128,2048]{2,1,0:T(8,128)S(1)}, f32[1,128,2048]{2,1,0:T(8,128)}, u32[]{:S(2)}) copy-start(f32[1,128,2048]{2,1,0:T(8,128)} %get-tuple-element.213) | copy-start | bytes 3145732 | tf_op jit(solution)/shard_map/while
  127.8 5.5 %copy-start = (f32[128,2048]{1,0:T(8,128)S(1)}, f32[128,2048]{1,0:T(8,128)}, u32[]{:S(2)}) copy-start(f32[128,2048]{1,0:T(8,128)} %get-tuple-element.214) | copy-start | bytes 3145732 | tf_op jit(solution)/shard_map/while
  127.8 5.5 %copy-start.1 = (f32[1,128,2048]{2,1,0:T(8,128)S(1)}, f32[1,128,2048]{2,1,0:T(8,128)}, u32[]{:S(2)}) copy-start(f32[1,128,2048]{2,1,0:T(8,128)} %get-tuple-element.213) | copy-start | bytes 3145732 | tf_op jit(solution)/shard_map/while
  151.7 5.5 %copy-start.1 = (f32[1,128,2048]{2,1,0:T(8,128)S(1)}, f32[1,128,2048]{2,1,0:T(8,128)}, u32[]{:S(2)}) copy-start(f32[1,128,2048]{2,1,0:T(8,128)} %get-tuple-element.213) | copy-start | bytes 3145732 | tf_op jit(solution)/shard_map/while
  175.7 5.5 %copy-start = (f32[128,2048]{1,0:T(8,128)S(1)}, f32[128,2048]{1,0:T(8,128)}, u32[]{:S(2)}) copy-start(f32[128,2048]{1,0:T(8,128)} %get-tuple-element.214) | copy-start | bytes 3145732 | tf_op jit(solution)/shard_map/while
  175.7 5.5 %copy-start.1 = (f32[1,128,2048]{2,1,0:T(8,128)S(1)}, f32[1,128,2048]{2,1,0:T(8,128)}, u32[]{:S(2)}) copy-start(f32[1,128,2048]{2,1,0:T(8,128)} %get-tuple-element.213) | copy-start | bytes 3145732 | tf_op jit(solution)/shard_map/while
  199.8 5.5 %copy-start = (f32[128,2048]{1,0:T(8,128)S(1)}, f32[128,2048]{1,0:T(8,128)}, u32[]{:S(2)}) copy-start(f32[128,2048]{1,0:T(8,128)} %get-tuple-element.214) | copy-start | bytes 3145732 | tf_op jit(solution)/shard_map/while
  199.8 5.5 %copy-start.1 = (f32[1,128,2048]{2,1,0:T(8,128)S(1)}, f32[1,128,2048]{2,1,0:T(8,128)}, u32[]{:S(2)}) copy-start(f32[1,128,2048]{2,1,0:T(8,128)} %get-tuple-element.213) | copy-start | bytes 3145732 | tf_op jit(solution)/shard_map/while
  224.0 5.5 %copy-start = (f32[128,2048]{1,0:T(8,128)S(1)}, f32[128,2048]{1,0:T(8,128)}, u32[]{:S(2)}) copy-start(f32[128,2048]{1,0:T(8,128)} %get-tuple-element.214) | copy-start | bytes 3145732 | tf_op jit(solution)/shard_map/while
  224.0 5.5 %copy-start.1 = (f32[1,128,2048]{2,1,0:T(8,128)S(1)}, f32[1,128,2048]{2,1,0:T(8,128)}, u32[]{:S(2)}) copy-start(f32[1,128,2048]{2,1,0:T(8,128)} %get-tuple-element.213) | copy-start | bytes 3145732 | tf_op jit(solution)/shard_map/while
  248.1 5.5 %copy-start.1 = (f32[1,128,2048]{2,1,0:T(8,128)S(1)}, f32[1,128,2048]{2,1,0:T(8,128)}, u32[]{:S(2)}) copy-start(f32[1,128,2048]{2,1,0:T(8,128)} %get-tuple-element.213) | copy-start | bytes 3145732 | tf_op jit(solution)/shard_map/while
  272.0 5.5 %copy-start = (f32[128,2048]{1,0:T(8,128)S(1)}, f32[128,2048]{1,0:T(8,128)}, u32[]{:S(2)}) copy-start(f32[128,2048]{1,0:T(8,128)} %get-tuple-element.214) | copy-start | bytes 3145732 | tf_op jit(solution)/shard_map/while
  272.0 5.5 %copy-start.1 = (f32[1,128,2048]{2,1,0:T(8,128)S(1)}, f32[1,128,2048]{2,1,0:T(8,128)}, u32[]{:S(2)}) copy-start(f32[1,128,2048]{2,1,0:T(8,128)} %get-tuple-element.213) | copy-start | bytes 3145732 | tf_op jit(solution)/shard_map/while
  296.2 5.5 %copy-start = (f32[128,2048]{1,0:T(8,128)S(1)}, f32[128,2048]{1,0:T(8,128)}, u32[]{:S(2)}) copy-start(f32[128,2048]{1,0:T(8,128)} %get-tuple-element.214) | copy-start | bytes 3145732 | tf_op jit(solution)/shard_map/while
  296.2 5.5 %copy-start.1 = (f32[1,128,2048]{2,1,0:T(8,128)S(1)}, f32[1,128,2048]{2,1,0:T(8,128)}, u32[]{:S(2)}) copy-start(f32[1,128,2048]{2,1,0:T(8,128)} %get-tuple-element.213) | copy-start | bytes 3145732 | tf_op jit(solution)/shard_map/while
  320.4 5.5 %copy-start = (f32[128,2048]{1,0:T(8,128)S(1)}, f32[128,2048]{1,0:T(8,128)}, u32[]{:S(2)}) copy-start(f32[128,2048]{1,0:T(8,128)} %get-tuple-element.214) | copy-start | bytes 3145732 | tf_op jit(solution)/shard_map/while
  320.4 5.5 %copy-start.1 = (f32[1,128,2048]{2,1,0:T(8,128)S(1)}, f32[1,128,2048]{2,1,0:T(8,128)}, u32[]{:S(2)}) copy-start(f32[1,128,2048]{2,1,0:T(8,128)} %get-tuple-element.213) | copy-start | bytes 3145732 | tf_op jit(solution)/shard_map/while
  344.2 5.5 %copy-start.1 = (f32[1,128,2048]{2,1,0:T(8,128)S(1)}, f32[1,128,2048]{2,1,0:T(8,128)}, u32[]{:S(2)}) copy-start(f32[1,128,2048]{2,1,0:T(8,128)} %get-tuple-element.213) | copy-start | bytes 3145732 | tf_op jit(solution)/shard_map/while
  368.1 5.5 %copy-start.1 = (f32[1,128,2048]{2,1,0:T(8,128)S(1)}, f32[1,128,2048]{2,1,0:T(8,128)}, u32[]{:S(2)}) copy-start(f32[1,128,2048]{2,1,0:T(8,128)} %get-tuple-element.213) | copy-start | bytes 3145732 | tf_op jit(solution)/shard_map/while
  392.1 5.5 %copy-start.1 = (f32[1,128,2048]{2,1,0:T(8,128)S(1)}, f32[1,128,2048]{2,1,0:T(8,128)}, u32[]{:S(2)}) copy-start(f32[1,128,2048]{2,1,0:T(8,128)} %get-tuple-element.213) | copy-start | bytes 3145732 | tf_op jit(solution)/shard_map/while
  416.0 5.5 %copy-start.1 = (f32[1,128,2048]{2,1,0:T(8,128)S(1)}, f32[1,128,2048]{2,1,0:T(8,128)}, u32[]{:S(2)}) copy-start(f32[1,128,2048]{2,1,0:T(8,128)} %get-tuple-element.213) | copy-start | bytes 3145732 | tf_op jit(solution)/shard_map/while
  440.0 5.5 %copy-start.1 = (f32[1,128,2048]{2,1,0:T(8,128)S(1)}, f32[1,128,2048]{2,1,0:T(8,128)}, u32[]{:S(2)}) copy-start(f32[1,128,2048]{2,1,0:T(8,128)} %get-tuple-element.213) | copy-start | bytes 3145732 | tf_op jit(solution)/shard_map/while
  457.5 4.8 collective-permute-start.4
  465.3 26.4 %collective-permute-start.5 = (f32[4,128,2,256]{3,1,2,0:T(8,128)S(1)}, f32[4,128,2,256]{3,1,2,0:T(8,128)}, u32[]{:S(2)}, u32[]{:S(2)}) collective-permute-start(f32[4,128,2,256]{3,1,2,0:T(8,128)S(1)} %fusion.25), channel_id=1, source_target_pairs={{0,32},{32,0},{16,48},{48,16},{64,96},{96,64},{80,112},{112,80},{1... | collective-permute-start | bytes 3145736 | tf_op jit(solution)/shard_map/ppermute | solution.py:34
  493.4 15.0 %collective-permute-start.6 = (f32[4,128,256]{2,1,0:T(8,128)S(1)}, f32[4,128,256]{2,1,0:T(8,128)S(1)}, u32[]{:S(2)}, u32[]{:S(2)}) collective-permute-start(f32[4,128,256]{2,1,0:T(8,128)S(1)} %fusion.30), channel_id=1, source_target_pairs={{0,64},{64,0},{16,80},{80,16},{32,96},{96,32},{48,112},{112,48},{1... | collective-permute-start | bytes 1572872 | tf_op jit(solution)/shard_map/ppermute | solution.py:34
  (41 other events, 222.9 us)
where the time goes:
time: 514 us; the launch traced here: 509 us
  other arithmetic  361 us (70%)
  local copies, waits for them, and re-layouts  56.9 us (11%)
  waiting for transfers between devices  40.6 us (8%)
  loops' own time  32 us (6%)
  starting transfers between devices  19.1 us (4%)
    mul x16, other arithmetic, shade(): return (opacity * lighting * colors, opacity)  218 us
    mul x16, other arithmetic, advance(): return ((color_sum + transmit * shaded, transmit * (1.0 - opacity)), None)  86.7 us
    ppermute x3, waiting for transfers between devices, swapped(): return lax.ppermute(block, axis, route)  37.4 us
    another operation x1, loops' own time, march(): lax.scan(advance, start_state, jnp.arange(depth_count, dtype=jnp.int32))  32 us
    add x16, other arithmetic, advance(): return ((color_sum + transmit * shaded, transmit * (1.0 - opacity)), None)  25.9 us
    unnamed x5, local copies, waits for them, and re-layouts  15.1 us
    slice x16, local copies, waits for them, and re-layouts, shade(): extinct = center * jax.nn.softplus(transfer[0, 3] * center + transfer[1, 3])  10.8 us
  transfers between devices with their start and end apart: 7, of which 5 were waited for; matrix products, arithmetic and copies ran while one was open for 2% of the time, Pallas kernels for 0%

commit v1 on v0

v1 whole, which is shorter than its diff:
```python
import functools

import jax
import jax.numpy as jnp
from jax import lax
from jax.experimental import pallas as pl
from jax.experimental.pallas import tpu as pltpu
from jax.sharding import PartitionSpec as P

MESH = pl.DeviceIdType.MESH
LOG2E = 1.4426950408889634
LANES = 128
PAD = 8
SLOTS = 12
CHUNKS = 8


def remote(src, dst, send_sem, recv_sem, **where):
    return pltpu.make_async_remote_copy(
        src_ref=src,
        dst_ref=dst,
        send_sem=send_sem,
        recv_sem=recv_sem,
        device_id=where,
        device_id_type=MESH,
    )


def blend(mine, theirs, mine_in_front):
    front = [jnp.where(mine_in_front, a, b) for a, b in zip(mine, theirs)]
    back = [jnp.where(mine_in_front, b, a) for a, b in zip(mine, theirs)]
    return [front[c] + front[3] * back[c] for c in range(3)] + [front[3] * back[3]]


def kernel(
    dims,
    occ,
    transfer,
    density,
    out,
    brick,
    z_recv,
    z_edge,
    flags,
    z_flags,
    y_send,
    y_recv,
    slots,
    keep1,
    send1,
    recv1,
    keep_a,
    send_a,
    recv_a,
    keep_b,
    send_b,
    recv_b,
    slot_block,
    left_of,
    right_of,
    slot_of,
    load_sem,
    z_sems,
    f_sems,
    y_sems,
    sems1,
    sems_a,
    sems_b,
):
    cells, rows, blocks, depth_n, rows_n = dims
    chunk_rows = rows // CHUNKS
    depth_at, row_at = lax.axis_index("depth"), lax.axis_index("rows")
    chip, core = depth_at // 2, depth_at % 2
    edge_chip = jnp.where(jnp.logical_or(chip == 0, chip == 3), 1, 0)
    sibling = depth_at + 1 - 2 * core
    pair_a = depth_at + 2 - 4 * (chip % 2)
    pair_b = (3 - chip) * 2 + core
    has_front, has_back = depth_at > 0, depth_at < depth_n - 1
    has_up, has_down = row_at > 0, row_at < rows_n - 1
    far = depth_at + 2 * core - 1
    has_far = jnp.logical_and(far >= 0, far < depth_n)

    loads = [
        pltpu.make_async_copy(
            density.at[:, :, pl.ds(LANES * b, LANES)],
            brick.at[b, :, pl.ds(PAD, rows), :],
            load_sem.at[b],
        )
        for b in range(blocks)
    ]
    for copy in loads:
        copy.start()

    barrier = pltpu.get_barrier_semaphore()

    def greet(**where):
        pl.semaphore_signal(barrier, inc=1, device_id=where, device_id_type=MESH)

    greet(depth=sibling)
    greet(depth=pair_a)
    greet(depth=pair_b)

    @pl.when(has_far)
    def _():
        greet(depth=far)

    @pl.when(has_up)
    def _():
        greet(rows=row_at - 1)

    @pl.when(has_down)
    def _():
        greet(rows=row_at + 1)

    peers = 3
    for condition in (has_far, has_up, has_down):
        peers = peers + jnp.where(condition, 1, 0)
    pl.semaphore_wait(barrier, peers)

    for b in range(blocks):
        flags[pl.ds(b, 1), :] = jnp.full((1, LANES), occ[0, 0, b], jnp.int32).astype(jnp.float32)

    def chunk_at(t):
        return lax.rem(t + 1, CHUNKS)

    def z_copy(side, c):
        span = pl.ds(pl.multiple_of(c * chunk_rows, chunk_rows), chunk_rows)
        return remote(
            density.at[cells - 1 if side == 0 else 0, span, :],
            z_recv.at[side, span, :],
            z_sems.at[0, side, c],
            z_sems.at[1, side, c],
            depth=depth_at + 1 if side == 0 else depth_at - 1,
        )

    def flag_copy(side):
        return remote(
            flags,
            z_flags.at[side],
            f_sems.at[0, side],
            f_sems.at[1, side],
            depth=depth_at + 1 if side == 0 else depth_at - 1,
        )

    def y_copy(side):
        return remote(
            y_send.at[side],
            y_recv.at[side],
            y_sems.at[0, side],
            y_sems.at[1, side],
            rows=row_at + 1 if side == 0 else row_at - 1,
        )

    z_sends, z_receives = (has_back, has_front), (has_front, has_back)
    y_sends, y_receives = (has_down, has_up), (has_up, has_down)

    for side in range(2):

        @pl.when(z_sends[side])
        def _(side=side):
            flag_copy(side).start()

    def start_halo(t, carry):
        for side in range(2):

            @pl.when(z_sends[side])
            def _(side=side):
                z_copy(side, chunk_at(t)).start()

        return carry

    lax.fori_loop(0, CHUNKS, start_halo, 0)

    occupied = [occ[0, 0, b] for b in range(blocks)]
    before, count = [], jnp.int32(0)
    for b in range(blocks):
        before.append(count)
        count = count + occupied[b]
    for s in range(SLOTS):
        found = jnp.int32(0)
        for b in range(1, blocks):
            hit = jnp.logical_and(occupied[b] == 1, before[b] == s)
            found = jnp.where(hit, b, found)
        slot_block[s] = found
    for b in range(blocks):
        slot_of[b] = jnp.where(occupied[b] == 1, before[b], SLOTS)
        left_of[b] = blocks if b == 0 else jnp.where(occupied[b - 1] == 1, b - 1, blocks)
        right_of[b] = (
            blocks if b == blocks - 1 else jnp.where(occupied[b + 1] == 1, b + 1, blocks)
        )

    def clear(z, carry):
        brick[blocks, z] = jnp.zeros(brick.shape[2:], jnp.float32)
        return carry

    lax.fori_loop(0, cells, clear, 0)
    for c in range(4):
        slots[c, SLOTS] = jnp.full((chunk_rows, LANES), float(c == 3), jnp.float32)
    for side in range(2):

        @pl.when(jnp.logical_not(z_receives[side]))
        def _(side=side):
            z_edge[side] = jnp.zeros(z_edge.shape[1:], jnp.float32)

    for copy in loads:
        copy.wait()

    def pack(b, carry):
        flag = flags[pl.ds(b, 1), :]
        for z in range(cells):
            y_send[0, b, pl.ds(z, 1), :] = brick[b, z, pl.ds(PAD + rows - 1, 1), :] * flag
            y_send[1, b, pl.ds(z, 1), :] = brick[b, z, pl.ds(PAD, 1), :] * flag
        return carry

    lax.fori_loop(0, blocks, pack, 0)
    for side in range(2):

        @pl.when(y_sends[side])
        def _(side=side):
            y_copy(side).start()

        @pl.when(z_receives[side])
        def _(side=side):
            flag_copy(side).wait_recv()

    halo_row = (PAD - 1, PAD + rows)

    def unpack():
        for side in range(2):

            @pl.when(y_receives[side])
            def _(side=side):
                y_copy(side).wait_recv()

                def one(b, carry):
                    for z in range(cells):
                        brick[b, z, pl.ds(halo_row[side], 1), :] = y_recv[side, b, pl.ds(z, 1), :]
                    return carry

                lax.fori_loop(0, blocks, one, 0)

            @pl.when(jnp.logical_not(y_receives[side]))
            def _(side=side):
                def one(b, carry):
                    for z in range(cells):
                        brick[b, z, pl.ds(halo_row[side], 1), :] = jnp.zeros(
                            (1, LANES), jnp.float32
                        )
                    return carry

                lax.fori_loop(0, blocks, one, 0)

    lane = lax.broadcasted_iota(jnp.int32, (chunk_rows, LANES), 1)
    first_lane, last_lane = lane == 0, lane == LANES - 1
    ext_slope, ext_offset = transfer[0, 3] * LOG2E, transfer[1, 3] * LOG2E
    step_scale = -2.0 / (cells * depth_n) * LOG2E
    channels = [(transfer[0, c] * 0.5, transfer[1, c] * 0.5) for c in range(3)]

    def march(s, first_row):
        b = slot_block[s]
        left, right = left_of[b], right_of[b]
        row = pl.multiple_of(PAD + first_row, 8)
        previous, center = z_edge[0, b], brick[b, 0, pl.ds(row, chunk_rows), :]
        transmit = jnp.ones((chunk_rows, LANES), jnp.float32)
        total = jnp.zeros((chunk_rows, LANES), jnp.float32)
        sums = [jnp.zeros((chunk_rows, LANES), jnp.float32) for _ in range(3)]
        for z in range(cells):
            following = (
                brick[b, z + 1, pl.ds(row, chunk_rows), :] if z + 1 < cells else z_edge[1, b]
            )
            diff_z = following - previous
            diff_y = (
                brick[b, z, pl.ds(row + 1, chunk_rows), :]
                - brick[b, z, pl.ds(row - 1, chunk_rows), :]
            )
            beside = brick[right, z, pl.ds(row, chunk_rows), :]
            after = pltpu.roll(jnp.where(first_lane, beside, center), LANES - 1, 1)
            beside = brick[left, z, pl.ds(row, chunk_rows), :]
            ahead = pltpu.roll(jnp.where(last_lane, beside, center), 1, 1)
            diff_x = after - ahead
            slope = jnp.abs(0.168 * diff_z + 0.21 * diff_y + 0.224 * diff_x)
            norm = diff_x * diff_x + diff_y * diff_y + (diff_z * diff_z + 4.0)
            lighting = 0.15 + slope * lax.rsqrt(norm)
            grown = 1.0 + jnp.exp2(ext_slope * center + ext_offset)
            kept = transmit * jnp.exp2((step_scale * center) * jnp.log(grown))
            weight = (transmit - kept) * lighting
            transmit = kept
            total = total + weight
            for c in range(3):
                slope_c, offset_c = channels[c]
                sums[c] = sums[c] + weight * jnp.tanh(slope_c * center + offset_c)
            previous, center = center, following
        for c in range(3):
            slots[c, s] = total + sums[c]
        slots[3, s] = transmit

    def copy1(c):
        return remote(
            send1.at[c], recv1.at[c], sems1.at[0, c], sems1.at[1, c], depth=sibling
        )

    def copy_a(c):
        return remote(
            send_a.at[c], recv_a.at[c], sems_a.at[0, c], sems_a.at[1, c], depth=pair_a
        )

    def copy_b(c):
        return remote(
            send_b.at[c], recv_b.at[c], sems_b.at[0, c], sems_b.at[1, c], depth=pair_b
        )

    def hand_over(c):
        for q in range(blocks // 2):
            theirs = slot_of[4 * (q // 2) + q % 2 + 2 * (1 - core)]
            mine = slot_of[4 * (q // 2) + q % 2 + 2 * core]
            for ch in range(4):
                send1[c, q, ch] = slots[ch, theirs]
        copy1(c).start()
        for q in range(blocks // 2):
            mine = slot_of[4 * (q // 2) + q % 2 + 2 * core]
            for ch in range(4):
                keep1[q, ch] = slots[ch, mine]

    def stage_a(c):
        copy1(c).wait_recv()

        def merged(q):
            return blend(
                [keep1[q, ch] for ch in range(4)],
                [recv1[c, q, ch] for ch in range(4)],
                core == 0,
            )

        for n in range(2):
            dest = n + n * 2 * (1 - edge_chip) + edge_chip
            for i in range(2):
                for ch, value in enumerate(merged(dest * 2 + i)):
                    send_a[c, n * 2 + i, ch] = value
        copy_a(c).start()
        for n in range(2):
            dest = n + n * 2 * edge_chip + (1 - edge_chip)
            for i in range(2):
                for ch, value in enumerate(merged(dest * 2 + i)):
                    keep_a[c, n * 2 + i, ch] = value

    def stage_b(c):
        copy_a(c).wait_recv()
        own = chip // 2

        def merged(p):
            return blend(
                [keep_a[c, p, ch] for ch in range(4)],
                [recv_a[c, p, ch] for ch in range(4)],
                chip % 2 == 0,
            )

        for i in range(2):
            for ch, value in enumerate(merged((1 - own) * 2 + i)):
                send_b[c, i, ch] = value
        copy_b(c).start()
        for i in range(2):
            for ch, value in enumerate(merged(own * 2 + i)):
                keep_b[c, i, ch] = value

    def finish(c):
        copy_b(c).wait_recv()
        span = pl.ds(pl.multiple_of(c * chunk_rows, chunk_rows), chunk_rows)
        for i in range(2):
            value = blend(
                [keep_b[c, i, ch] for ch in range(4)],
                [recv_b[c, i, ch] for ch in range(4)],
                chip < 2,
            )
            value[3] = 1.0 - value[3]
            for ch in range(4):
                out[ch, span, pl.ds(i * LANES, LANES)] = value[ch]

    lag_a, lag_b, lag_f = 1, 2, 3

    def one_chunk(t, carry):
        c = chunk_at(t)
        first_row = pl.multiple_of(c * chunk_rows, chunk_rows)

        @pl.when(t == CHUNKS - 2)
        def _():
            unpack()

        for side in range(2):

            @pl.when(z_receives[side])
            def _(side=side):
                z_copy(side, c).wait_recv()
                for b in range(blocks):
                    layer = z_recv[
                        side, pl.ds(first_row, chunk_rows), pl.ds(b * LANES, LANES)
                    ]
                    z_edge[side, b] = layer * z_flags[side, pl.ds(b, 1), :]

        def one_slot(s, inner):
            march(s, first_row)

            @pl.when(jnp.logical_and(s == 3, t >= lag_a))
            def _():
                stage_a(chunk_at(t - lag_a))

            @pl.when(jnp.logical_and(s == 7, t >= lag_b))
            def _():
                stage_b(chunk_at(t - lag_b))

            @pl.when(jnp.logical_and(s == 9, t >= lag_f))
            def _():
                finish(chunk_at(t - lag_f))

            return inner

        lax.fori_loop(0, SLOTS, one_slot, 0)
        hand_over(c)
        return carry

    lax.fori_loop(0, CHUNKS, one_chunk, 0)

    def tail(t, carry):
        @pl.when(t - lag_a < CHUNKS)
        def _():
            stage_a(chunk_at(t - lag_a))

        @pl.when(t - lag_b < CHUNKS)
        def _():
            stage_b(chunk_at(t - lag_b))

        finish(chunk_at(t - lag_f))
        return carry

    lax.fori_loop(CHUNKS, CHUNKS + lag_f, tail, 0)

    for side in range(2):

        @pl.when(z_sends[side])
        def _(side=side):
            flag_copy(side).wait_send()

        @pl.when(y_sends[side])
        def _(side=side):
            y_copy(side).wait_send()

    def drain(c, carry):
        for side in range(2):

            @pl.when(z_sends[side])
            def _(side=side):
                z_copy(side, c).wait_send()

        copy1(c).wait_send()
        copy_a(c).wait_send()
        copy_b(c).wait_send()
        return carry

    lax.fori_loop(0, CHUNKS, drain, 0)


def solution(mesh):
    depth_n, rows_n = mesh.shape["depth"], mesh.shape["rows"]

    def shards(density, occupancy, transfer):
        cells, rows, columns = density.shape
        blocks = columns // LANES
        chunk_rows = rows // CHUNKS
        half, quarter, eighth = blocks // 2, blocks // 4, blocks // 8
        f32 = jnp.float32
        tile = (chunk_rows, LANES)
        dma = pltpu.SemaphoreType.DMA
        return pl.pallas_call(
            functools.partial(kernel, (cells, rows, blocks, depth_n, rows_n)),
            out_shape=jax.ShapeDtypeStruct((4, rows, columns // depth_n), f32),
            in_specs=[
                pl.BlockSpec(memory_space=pltpu.SMEM),
                pl.BlockSpec(memory_space=pltpu.SMEM),
                pl.BlockSpec(memory_space=pl.ANY),
            ],
            out_specs=pl.BlockSpec(memory_space=pltpu.VMEM),
            scratch_shapes=[
                pltpu.VMEM((blocks + 1, cells, rows + 2 * PAD, LANES), f32),
                pltpu.VMEM((2, rows, columns), f32),
                pltpu.VMEM((2, blocks) + tile, f32),
                pltpu.VMEM((blocks, LANES), f32),
                pltpu.VMEM((2, blocks, LANES), f32),
                pltpu.VMEM((2, blocks, cells, LANES), f32),
                pltpu.VMEM((2, blocks, cells, LANES), f32),
                pltpu.VMEM((4, SLOTS + 1) + tile, f32),
                pltpu.VMEM((half, 4) + tile, f32),
                pltpu.VMEM((CHUNKS, half, 4) + tile, f32),
                pltpu.VMEM((CHUNKS, half, 4) + tile, f32),
                pltpu.VMEM((CHUNKS, quarter, 4) + tile, f32),
                pltpu.VMEM((CHUNKS, quarter, 4) + tile, f32),
                pltpu.VMEM((CHUNKS, quarter, 4) + tile, f32),
                pltpu.VMEM((CHUNKS, eighth, 4) + tile, f32),
                pltpu.VMEM((CHUNKS, eighth, 4) + tile, f32),
                pltpu.VMEM((CHUNKS, eighth, 4) + tile, f32),
                pltpu.SMEM((SLOTS,), jnp.int32),
                pltpu.SMEM((blocks,), jnp.int32),
                pltpu.SMEM((blocks,), jnp.int32),
                pltpu.SMEM((blocks,), jnp.int32),
                dma((blocks,)),
                dma((2, 2, CHUNKS)),
                dma((2, 2)),
                dma((2, 2)),
                dma((2, CHUNKS)),
                dma((2, CHUNKS)),
                dma((2, CHUNKS)),
            ],
            compiler_params=pltpu.CompilerParams(
                collective_id=0,
                has_side_effects=True,
                vmem_limit_bytes=56 * 2**20,
            ),
        )(occupancy, transfer, density)

    return jax.shard_map(
        shards,
        mesh=mesh,
        in_specs=(P("depth", "rows", None), P("depth", "rows", None), P()),
        out_specs=P(None, "rows", "depth"),
        check_vma=False,
    )
```

time: 514 us -> 57.6 us (0.11)
  other arithmetic: 361 us -> 0 us
  Pallas kernels: 0 us -> 55.5 us
  local copies, waits for them, and re-layouts: 56.9 us -> 1.87 us
  waiting for transfers between devices: 40.6 us -> 0 us
  loops' own time: 32 us -> 0 us
  starting transfers between devices: 19.1 us -> 0 us
    mul x37 -> x0, other arithmetic: 315 us -> none  [the longest x16 218 us: shade(): return (opacity * lighting * colors, opacity)]
    pallas_call x0 -> x1, Pallas kernels: none -> 55.5 us  [shards(): pl.pallas_call(functools.partial(kernel, (cells, rows, blocks, depth_n, r...]
    ppermute x7 -> x0, waiting for transfers between devices: 40.6 us -> none  [the longest x3 37.4 us: swapped(): return lax.ppermute(block, axis, route)]
    another operation x1 -> x0, loops' own time: 32 us -> none  [march(): lax.scan(advance, start_state, jnp.arange(depth_count, dtype=jnp.int32))]
    add x19 -> x0, other arithmetic: 26.3 us -> none  [the longest x16 25.9 us: advance(): return ((color_sum + transmit * shaded, transmit * (1.0 - opacity)), None)]
    ppermute x7 -> x0, starting transfers between devices: 19.1 us -> none  [the longest x3 6.96 us: swapped(): return lax.ppermute(block, axis, route)]
    concatenate x3 -> x0, other arithmetic: 14.6 us -> none  [the longest x1 10.1 us: with_halo(): jnp.concatenate([jnp.pad(low, around), x, jnp.pad(high, around)], axis=dim)]
    dynamic_slice x18 -> x0, local copies, waits for them, and re-layouts: 14.1 us -> none  [the longest x16 9.38 us: march(): lax.scan(advance, start_state, jnp.arange(depth_count, dtype=jnp.int32))]
  transfers between devices with their start and end apart: 7 -> 0, of which waited for: 5 -> 0; matrix products, arithmetic and copies ran while one was open for 2% -> 0% of each run, Pallas kernels for 0% -> 0%
where the time goes in v1:
time: 57.6 us; the launch traced here: 57.4 us
  Pallas kernels  55.5 us (96%)
  local copies, waits for them, and re-layouts  1.87 us (3%)
    pallas_call x1, Pallas kernels, shards(): pl.pallas_call(functools.partial(kernel, (cells, rows, blocks, depth_n, r...  55.5 us
    unnamed x1, local copies, waits for them, and re-layouts  1.87 us

profile of v1, /device:TPU:24, one launch (start us, length us, event | category | flops | bytes accessed | tf_op | source)
XLA Modules:
  0.0 57.4 jit_solution(5529730487960441132)
XLA Ops:
  0.0 55.5 %shard_map.37 = f32[4,128,256]{2,1,0:T(8,128)} custom-call(s32[1,1,16]{2,1,0:T(1,128)} %occ.1, f32[2,4]{1,0:T(2,128)} %transfer.1, f32[16,128,2048]{2,1,0:T(8,128)} %density.1), custom_call_target="tpu_custom_call" | custom-call | tf_op jit(solution)/shard_map/pallas_call | solution.py:472
  55.5 1.9 %copy.5 = f32[4,128,256]{2,1,0:T(8,128)} copy(f32[4,128,256]{2,1,0:T(8,128)} %shard_map.37) | data formatting | bytes 1048576

commit v2 on v1

v2 whole, which is shorter than its diff:
```python
import functools

import jax
import jax.numpy as jnp
from jax import lax
from jax.experimental import pallas as pl
from jax.experimental.pallas import tpu as pltpu
from jax.sharding import PartitionSpec as P

MESH = pl.DeviceIdType.MESH
LOG2E = 1.4426950408889634
LANES = 128
PAD = 8
SLOTS = 12
CHUNKS = 8
AHEAD = 2
GROUP = 2
LIGHT_SCALE = 0.224
LIGHT_FLOOR = 0.15 / LIGHT_SCALE


def remote(src, dst, send_sem, recv_sem, **where):
    return pltpu.make_async_remote_copy(
        src_ref=src,
        dst_ref=dst,
        send_sem=send_sem,
        recv_sem=recv_sem,
        device_id=where,
        device_id_type=MESH,
    )


def blend(mine, theirs, mine_in_front):
    front = [jnp.where(mine_in_front, a, b) for a, b in zip(mine, theirs)]
    back = [jnp.where(mine_in_front, b, a) for a, b in zip(mine, theirs)]
    return [front[c] + front[3] * back[c] for c in range(3)] + [front[3] * back[3]]


def kernel(
    dims,
    occ,
    transfer,
    density,
    out,
    brick,
    window,
    z_recv,
    z_edge,
    flags,
    z_flags,
    y_send,
    y_recv,
    slots,
    keep1,
    send1,
    recv1,
    send2,
    recv2,
    slot_block,
    left_of,
    right_of,
    slot_of,
    load_sem,
    window_sem,
    z_sems,
    f_sems,
    y_sems,
    sems1,
    sems2,
):
    cells, rows, blocks, depth_n, rows_n = dims
    chunk_rows = rows // CHUNKS
    depth_at, row_at = lax.axis_index("depth"), lax.axis_index("rows")
    chip, core = depth_at // 2, depth_at % 2
    sibling = depth_at + 1 - 2 * core
    has_front, has_back = depth_at > 0, depth_at < depth_n - 1
    has_up, has_down = row_at > 0, row_at < rows_n - 1
    far = depth_at + 2 * core - 1
    has_far = jnp.logical_and(far >= 0, far < depth_n)

    window_row = chunk_rows - PAD
    window_loads = [
        pltpu.make_async_copy(
            density.at[:, pl.ds(window_row, window.shape[2]), pl.ds(LANES * b, LANES)],
            window.at[b],
            window_sem.at[b],
        )
        for b in range(blocks)
    ]
    loads = [
        pltpu.make_async_copy(
            density.at[:, :, pl.ds(LANES * b, LANES)],
            brick.at[b, :, pl.ds(PAD, rows), :],
            load_sem.at[b],
        )
        for b in range(blocks)
    ]
    for copy in window_loads + loads:
        copy.start()

    barrier = pltpu.get_barrier_semaphore()

    def greet(**where):
        pl.semaphore_signal(barrier, inc=1, device_id=where, device_id_type=MESH)

    greet(depth=sibling)
    for offset in range(1, 4):
        greet(depth=lax.rem(depth_at + 2 * offset, depth_n))

    @pl.when(has_far)
    def _():
        greet(depth=far)

    @pl.when(has_up)
    def _():
        greet(rows=row_at - 1)

    @pl.when(has_down)
    def _():
        greet(rows=row_at + 1)

    for b in range(blocks):
        flags[pl.ds(b, 1), :] = jnp.full((1, LANES), occ[0, 0, b], jnp.int32).astype(jnp.float32)

    def chunk_at(t):
        return lax.rem(t + 1, CHUNKS)

    def z_copy(side, c):
        span = pl.ds(pl.multiple_of(c * chunk_rows, chunk_rows), chunk_rows)
        return remote(
            density.at[cells - 1 if side == 0 else 0, span, :],
            z_recv.at[side, span, :],
            z_sems.at[0, side, c],
            z_sems.at[1, side, c],
            depth=depth_at + 1 if side == 0 else depth_at - 1,
        )

    def flag_copy(side):
        return remote(
            flags,
            z_flags.at[side],
            f_sems.at[0, side],
            f_sems.at[1, side],
            depth=depth_at + 1 if side == 0 else depth_at - 1,
        )

    def y_copy(side):
        return remote(
            y_send.at[side],
            y_recv.at[side],
            y_sems.at[0, side],
            y_sems.at[1, side],
            rows=row_at + 1 if side == 0 else row_at - 1,
        )

    z_sends, z_receives = (has_back, has_front), (has_front, has_back)
    y_sends, y_receives = (has_down, has_up), (has_up, has_down)

    occupied = [occ[0, 0, b] for b in range(blocks)]
    before, count = [], jnp.int32(0)
    for b in range(blocks):
        before.append(count)
        count = count + occupied[b]
    for s in range(SLOTS):
        found = jnp.int32(0)
        for b in range(1, blocks):
            hit = jnp.logical_and(occupied[b] == 1, before[b] == s)
            found = jnp.where(hit, b, found)
        slot_block[s] = found
    for b in range(blocks):
        slot_of[b] = jnp.where(occupied[b] == 1, before[b], SLOTS)
        left_of[b] = blocks if b == 0 else jnp.where(occupied[b - 1] == 1, b - 1, blocks)
        right_of[b] = (
            blocks if b == blocks - 1 else jnp.where(occupied[b + 1] == 1, b + 1, blocks)
        )

    def clear(z, carry):
        brick[blocks, z] = jnp.zeros(brick.shape[2:], jnp.float32)
        window[blocks, z] = jnp.zeros(window.shape[2:], jnp.float32)
        return carry

    lax.fori_loop(0, cells, clear, 0)
    for r in range(AHEAD + 1):
        for c in range(4):
            slots[r, c, SLOTS] = jnp.full((chunk_rows, LANES), float(c == 3), jnp.float32)
    for side in range(2):

        @pl.when(jnp.logical_not(z_receives[side]))
        def _(side=side):
            z_edge[side] = jnp.zeros(z_edge.shape[1:], jnp.float32)

    halo_row = (PAD - 1, PAD + rows)

    def unpack():
        for side in range(2):

            @pl.when(y_receives[side])
            def _(side=side):
                y_copy(side).wait_recv()

                def one(b, carry):
                    for z in range(cells):
                        brick[b, z, pl.ds(halo_row[side], 1), :] = y_recv[side, b, pl.ds(z, 1), :]
                    return carry

                lax.fori_loop(0, blocks, one, 0)

            @pl.when(jnp.logical_not(y_receives[side]))
            def _(side=side):
                def one(b, carry):
                    for z in range(cells):
                        brick[b, z, pl.ds(halo_row[side], 1), :] = jnp.zeros(
                            (1, LANES), jnp.float32
                        )
                    return carry

                lax.fori_loop(0, blocks, one, 0)

    lane = lax.broadcasted_iota(jnp.int32, (chunk_rows, LANES), 1)
    first_lane, last_lane = lane == 0, lane == LANES - 1
    ext_slope, ext_offset = transfer[0, 3] * LOG2E, transfer[1, 3] * LOG2E
    step_scale = -2.0 / (cells * depth_n) * LOG2E
    channels = [(transfer[0, c] * 0.5, transfer[1, c] * 0.5) for c in range(3)]

    def shade(center, diff_z, diff_y, beside_left, beside_right, transmit):
        after = pltpu.roll(jnp.where(first_lane, beside_right, center), LANES - 1, 1)
        ahead = pltpu.roll(jnp.where(last_lane, beside_left, center), 1, 1)
        diff_x = after - ahead
        slope = jnp.abs(0.75 * diff_z + 0.9375 * diff_y + diff_x)
        norm = diff_x * diff_x + diff_y * diff_y + (diff_z * diff_z + 4.0)
        lighting = LIGHT_FLOOR + slope * lax.rsqrt(norm)
        grown = 1.0 + jnp.exp2(ext_slope * center + ext_offset)
        factor = jnp.exp2((step_scale * center) * jnp.log(grown))
        kept = factor if transmit is None else transmit * factor
        weight = ((1.0 if transmit is None else transmit) - kept) * lighting
        return kept, weight, [jnp.tanh(slope_c * center + offset_c) for slope_c, offset_c in channels]

    def cell_rows(ref, b, z, row):
        return ref[b, z, pl.ds(row, chunk_rows), :]

    def layer(ref, b, z, row, center, diff_z, transmit):
        diff_y = cell_rows(ref, b, z, row + 1) - cell_rows(ref, b, z, row - 1)
        return shade(
            center,
            diff_z,
            diff_y,
            cell_rows(ref, left_of[b], z, row),
            cell_rows(ref, right_of[b], z, row),
            transmit,
        )

    def march(ref, ring, first_slot, row):
        group = range(GROUP)
        block = [slot_block[first_slot + g] for g in group]
        previous = [cell_rows(ref, block[g], 0, row) for g in group]
        center = [cell_rows(ref, block[g], 1, row) for g in group]
        transmit, total, sums = [None] * GROUP, [None] * GROUP, [None] * GROUP
        for z in range(1, cells - 1):
            for g in group:
                following = cell_rows(ref, block[g], z + 1, row)
                kept, weight, factors = layer(
                    ref, block[g], z, row, center[g], following - previous[g], transmit[g]
                )
                products = [weight * f for f in factors]
                if total[g] is None:
                    total[g], sums[g] = weight, products
                else:
                    total[g] = total[g] + weight
                    sums[g] = [a + b for a, b in zip(sums[g], products)]
                transmit[g] = kept
                previous[g], center[g] = center[g], following
        for g in group:
            for c in range(3):
                slots[ring, c, first_slot + g] = LIGHT_SCALE * (total[g] + sums[g][c])
            slots[ring, 3, first_slot + g] = transmit[g]

    def ends(ring, first_slot, row):
        for g in range(GROUP):
            s = first_slot + g
            b = slot_block[s]
            color = [slots[ring, c, s] for c in range(3)]
            last = cells - 1
            center = cell_rows(brick, b, 0, row)
            diff_z = cell_rows(brick, b, 1, row) - z_edge[0, b]
            kept, weight, factors = layer(brick, b, 0, row, center, diff_z, None)
            weight = weight * LIGHT_SCALE
            color = [(weight + weight * f) + kept * c for f, c in zip(factors, color)]
            transmit = kept * slots[ring, 3, s]
            center = cell_rows(brick, b, last, row)
            diff_z = z_edge[1, b] - cell_rows(brick, b, last - 1, row)
            kept, weight, factors = layer(brick, b, last, row, center, diff_z, transmit)
            weight = weight * LIGHT_SCALE
            for c in range(3):
                slots[ring, c, s] = color[c] + (weight + weight * factors[c])
            slots[ring, 3, s] = kept

    def copy1(c):
        return remote(
            send1.at[c], recv1.at[c], sems1.at[0, c], sems1.at[1, c], depth=sibling
        )

    def copy2(c, offset):
        dest = lax.rem(chip + offset, 4)
        return remote(
            send2.at[c, dest],
            recv2.at[c, offset],
            sems2.at[0, offset - 1, c],
            sems2.at[1, offset - 1, c],
            depth=2 * dest + core,
        )

    def hand_over(c, ring):
        for q in range(blocks // 2):
            theirs = slot_of[4 * (q // 2) + q % 2 + 2 * (1 - core)]
            for ch in range(4):
                send1[c, q, ch] = slots[ring, ch, theirs]
        copy1(c).start()
        for q in range(blocks // 2):
            mine = slot_of[4 * (q // 2) + q % 2 + 2 * core]
            for ch in range(4):
                keep1[c, q, ch] = slots[ring, ch, mine]

    def merge(c):
        copy1(c).wait_recv()

        def merged(q):
            return blend(
                [keep1[c, q, ch] for ch in range(4)],
                [recv1[c, q, ch] for ch in range(4)],
                core == 0,
            )

        for offset in (2, 1, 3):
            dest = lax.rem(chip + offset, 4)
            for i in range(2):
                for ch, value in enumerate(merged(2 * dest + i)):
                    send2[c, dest, i, ch] = value
            copy2(c, offset).start()
        for i in range(2):
            for ch, value in enumerate(merged(2 * chip + i)):
                recv2[c, 0, i, ch] = value

    def finish(t, carry):
        c = chunk_at(t)
        for offset in range(1, 4):
            copy2(c, offset).wait_recv()
        span = pl.ds(pl.multiple_of(c * chunk_rows, chunk_rows), chunk_rows)
        for i in range(2):
            value = None
            for source in (3, 2, 1, 0):
                offset = lax.rem(chip - source + 4, 4)
                part = [recv2[c, offset, i, ch] for ch in range(4)]
                if value is None:
                    value = part
                else:
                    value = [part[k] + part[3] * value[k] for k in range(3)] + [part[3] * value[3]]
            value[3] = 1.0 - value[3]
            for ch in range(4):
                out[ch, span, pl.ds(i * LANES, LANES)] = value[ch]
        return carry

    def march_window(t):
        def one(s, carry):
            march(window, t, s * GROUP, PAD + t * chunk_rows)
            return carry

        lax.fori_loop(0, SLOTS // GROUP, one, 0)

    for copy in window_loads:
        copy.wait()
    march_window(0)
    peers = 4
    for condition in (has_far, has_up, has_down):
        peers = peers + jnp.where(condition, 1, 0)
    pl.semaphore_wait(barrier, peers)

    for side in range(2):

        @pl.when(z_sends[side])
        def _(side=side):
            flag_copy(side).start()

    def start_halo(t, carry):
        for side in range(2):

            @pl.when(z_sends[side])
            def _(side=side):
                z_copy(side, chunk_at(t)).start()

        return carry

    lax.fori_loop(0, CHUNKS, start_halo, 0)

    march_window(1)

    for copy in loads:
        copy.wait()

    def pack(b, carry):
        flag = flags[pl.ds(b, 1), :]
        for z in range(cells):
            y_send[0, b, pl.ds(z, 1), :] = brick[b, z, pl.ds(PAD + rows - 1, 1), :] * flag
            y_send[1, b, pl.ds(z, 1), :] = brick[b, z, pl.ds(PAD, 1), :] * flag
        return carry

    lax.fori_loop(0, blocks, pack, 0)
    for side in range(2):

        @pl.when(y_sends[side])
        def _(side=side):
            y_copy(side).start()

        @pl.when(z_receives[side])
        def _(side=side):
            flag_copy(side).wait_recv()

    def one_chunk(t, carry):
        c = chunk_at(t)
        first_row = pl.multiple_of(c * chunk_rows, chunk_rows)
        for side in range(2):

            @pl.when(z_receives[side])
            def _(side=side):
                z_copy(side, c).wait_recv()
                for b in range(blocks):
                    edge = z_recv[side, pl.ds(first_row, chunk_rows), pl.ds(b * LANES, LANES)]
                    z_edge[side, b] = edge * z_flags[side, pl.ds(b, 1), :]

        ring = lax.rem(t, AHEAD + 1)
        row = pl.multiple_of(PAD + first_row, 8)

        def one_end(s, inner):
            ends(ring, s * GROUP, row)
            return inner

        lax.fori_loop(0, SLOTS // GROUP, one_end, 0)
        hand_over(c, ring)

        @pl.when(t == CHUNKS - 2 - AHEAD)
        def _():
            unpack()

        @pl.when(t + AHEAD < CHUNKS)
        def _():
            later_ring = lax.rem(t + AHEAD, AHEAD + 1)
            later_row = pl.multiple_of(PAD + chunk_at(t + AHEAD) * chunk_rows, 8)

            def one_slot(s, inner):
                march(brick, later_ring, s * GROUP, later_row)

                @pl.when(s == SLOTS // GROUP - 2)
                def _():
                    merge(c)

                return inner

            lax.fori_loop(0, SLOTS // GROUP, one_slot, 0)

        return carry

    lax.fori_loop(0, CHUNKS, one_chunk, 0)
    for t in range(CHUNKS - AHEAD, CHUNKS):
        merge(chunk_at(t))
    lax.fori_loop(0, CHUNKS, finish, 0)

    for side in range(2):

        @pl.when(z_sends[side])
        def _(side=side):
            flag_copy(side).wait_send()

        @pl.when(y_sends[side])
        def _(side=side):
            y_copy(side).wait_send()

    def drain(c, carry):
        for side in range(2):

            @pl.when(z_sends[side])
            def _(side=side):
                z_copy(side, c).wait_send()

        copy1(c).wait_send()
        for offset in range(1, 4):
            copy2(c, offset).wait_send()
        return carry

    lax.fori_loop(0, CHUNKS, drain, 0)


def solution(mesh):
    depth_n, rows_n = mesh.shape["depth"], mesh.shape["rows"]

    def shards(density, occupancy, transfer):
        cells, rows, columns = density.shape
        blocks = columns // LANES
        chunk_rows = rows // CHUNKS
        half = blocks // 2
        f32 = jnp.float32
        tile = (chunk_rows, LANES)
        dma = pltpu.SemaphoreType.DMA
        return pl.pallas_call(
            functools.partial(kernel, (cells, rows, blocks, depth_n, rows_n)),
            out_shape=jax.ShapeDtypeStruct((4, rows, columns // depth_n), f32),
            in_specs=[
                pl.BlockSpec(memory_space=pltpu.SMEM),
                pl.BlockSpec(memory_space=pltpu.SMEM),
                pl.BlockSpec(memory_space=pl.ANY),
            ],
            out_specs=pl.BlockSpec(memory_space=pltpu.VMEM),
            scratch_shapes=[
                pltpu.VMEM((blocks + 1, cells, rows + 2 * PAD, LANES), f32),
                pltpu.VMEM((blocks + 1, cells, AHEAD * chunk_rows + 2 * PAD, LANES), f32),
                pltpu.VMEM((2, rows, columns), f32),
                pltpu.VMEM((2, blocks) + tile, f32),
                pltpu.VMEM((blocks, LANES), f32),
                pltpu.VMEM((2, blocks, LANES), f32),
                pltpu.VMEM((2, blocks, cells, LANES), f32),
                pltpu.VMEM((2, blocks, cells, LANES), f32),
                pltpu.VMEM((AHEAD + 1, 4, SLOTS + 1) + tile, f32),
                pltpu.VMEM((CHUNKS, half, 4) + tile, f32),
                pltpu.VMEM((CHUNKS, half, 4) + tile, f32),
                pltpu.VMEM((CHUNKS, half, 4) + tile, f32),
                pltpu.VMEM((CHUNKS, 4, 2, 4) + tile, f32),
                pltpu.VMEM((CHUNKS, 4, 2, 4) + tile, f32),
                pltpu.SMEM((SLOTS,), jnp.int32),
                pltpu.SMEM((blocks,), jnp.int32),
                pltpu.SMEM((blocks,), jnp.int32),
                pltpu.SMEM((blocks,), jnp.int32),
                dma((blocks,)),
                dma((blocks,)),
                dma((2, 2, CHUNKS)),
                dma((2, 2)),
                dma((2, 2)),
                dma((2, CHUNKS)),
                dma((2, 3, CHUNKS)),
            ],
            compiler_params=pltpu.CompilerParams(
                collective_id=0,
                has_side_effects=True,
                vmem_limit_bytes=60 * 2**20,
            ),
        )(occupancy, transfer, density)

    return jax.shard_map(
        shards,
        mesh=mesh,
        in_specs=(P("depth", "rows", None), P("depth", "rows", None), P()),
        out_specs=P(None, "rows", "depth"),
        check_vma=False,
    )
```

time: 57.6 us -> 48.7 us (0.85)
  the two profiles are of different devices: /device:TPU:24 before, /device:TPU:1 now
where the time goes in v2:
time: 48.7 us; the launch traced here: 48.6 us
  Pallas kernels  46.7 us (96%)
  local copies, waits for them, and re-layouts  1.87 us (4%)
    pallas_call x1, Pallas kernels, shards(): pl.pallas_call(functools.partial(kernel, (cells, rows, blocks, depth_n, r...  46.7 us
    unnamed x1, local copies, waits for them, and re-layouts  1.87 us

profile of v2, /device:TPU:1, one launch (start us, length us, event | category | flops | bytes accessed | tf_op | source)
XLA Modules:
  0.0 48.6 jit_solution(281351531375215732)
XLA Ops:
  0.0 46.7 %shard_map.37 = f32[4,128,256]{2,1,0:T(8,128)} custom-call(s32[1,1,16]{2,1,0:T(1,128)} %occ.1, f32[2,4]{1,0:T(2,128)} %transfer.1, f32[16,128,2048]{2,1,0:T(8,128)} %density.1), custom_call_target="tpu_custom_call" | custom-call | tf_op jit(solution)/shard_map/pallas_call | solution.py:502
  46.7 1.9 %copy.5 = f32[4,128,256]{2,1,0:T(8,128)} copy(f32[4,128,256]{2,1,0:T(8,128)} %shard_map.37) | data formatting | bytes 1048576

commit v3 on v2

--- a/solution.py
+++ b/solution.py
@@ -14,7 +14,7 @@
 SLOTS = 12
 CHUNKS = 8
 AHEAD = 2
-GROUP = 2
+GROUP = 4
 LIGHT_SCALE = 0.224
 LIGHT_FLOOR = 0.15 / LIGHT_SCALE
 
@@ -78,6 +78,27 @@
     far = depth_at + 2 * core - 1
     has_far = jnp.logical_and(far >= 0, far < depth_n)
 
+    barrier = pltpu.get_barrier_semaphore()
+
+    def greet(**where):
+        pl.semaphore_signal(barrier, inc=1, device_id=where, device_id_type=MESH)
+
+    greet(depth=sibling)
+    for offset in range(1, 4):
+        greet(depth=lax.rem(depth_at + 2 * offset, depth_n))
+
+    @pl.when(has_far)
+    def _():
+        greet(depth=far)
+
+    @pl.when(has_up)
+    def _():
+        greet(rows=row_at - 1)
+
+    @pl.when(has_down)
+    def _():
+        greet(rows=row_at + 1)
+
     window_row = chunk_rows - PAD
     window_loads = [
         pltpu.make_async_copy(
@@ -95,29 +116,8 @@
         )
         for b in range(blocks)
     ]
-    for copy in window_loads + loads:
+    for copy in window_loads:
         copy.start()
-
-    barrier = pltpu.get_barrier_semaphore()
-
-    def greet(**where):
-        pl.semaphore_signal(barrier, inc=1, device_id=where, device_id_type=MESH)
-
-    greet(depth=sibling)
-    for offset in range(1, 4):
-        greet(depth=lax.rem(depth_at + 2 * offset, depth_n))
-
-    @pl.when(has_far)
-    def _():
-        greet(depth=far)
-
-    @pl.when(has_up)
-    def _():
-        greet(rows=row_at - 1)
-
-    @pl.when(has_down)
-    def _():
-        greet(rows=row_at + 1)
 
     for b in range(blocks):
         flags[pl.ds(b, 1), :] = jnp.full((1, LANES), occ[0, 0, b], jnp.int32).astype(jnp.float32)
@@ -366,9 +366,6 @@
 
         lax.fori_loop(0, SLOTS // GROUP, one, 0)
 
-    for copy in window_loads:
-        copy.wait()
-    march_window(0)
     peers = 4
     for condition in (has_far, has_up, has_down):
         peers = peers + jnp.where(condition, 1, 0)
@@ -391,6 +388,11 @@
 
     lax.fori_loop(0, CHUNKS, start_halo, 0)
 
+    for copy in window_loads:
+        copy.wait()
+    for copy in loads:
+        copy.start()
+    march_window(0)
     march_window(1)
 
     for copy in loads:

time: 48.7 us -> 45.8 us (0.940)
  the two profiles are of different devices: /device:TPU:1 before, /device:TPU:24 now
where the time goes in v3:
time: 45.8 us; the launch traced here: 45.1 us
  Pallas kernels  43.2 us (94%)
  local copies, waits for them, and re-layouts  1.87 us (4%)
    pallas_call x1, Pallas kernels, shards(): pl.pallas_call(functools.partial(kernel, (cells, rows, blocks, depth_n, r...  43.2 us
    unnamed x1, local copies, waits for them, and re-layouts  1.87 us

profile of v3, /device:TPU:24, one launch (start us, length us, event | category | flops | bytes accessed | tf_op | source)
XLA Modules:
  0.0 45.1 jit_solution(4591807647999048916)
XLA Ops:
  0.0 43.2 %shard_map.37 = f32[4,128,256]{2,1,0:T(8,128)} custom-call(s32[1,1,16]{2,1,0:T(1,128)} %occ.1, f32[2,4]{1,0:T(2,128)} %transfer.1, f32[16,128,2048]{2,1,0:T(8,128)} %density.1), custom_call_target="tpu_custom_call" | custom-call | tf_op jit(solution)/shard_map/pallas_call | solution.py:504
  43.2 1.9 %copy.5 = f32[4,128,256]{2,1,0:T(8,128)} copy(f32[4,128,256]{2,1,0:T(8,128)} %shard_map.37) | data formatting | bytes 1048576

commit v4 on v3

--- a/solution.py
+++ b/solution.py
@@ -38,8 +38,8 @@
 
 def kernel(
     dims,
-    occ,
-    transfer,
+    occ_hbm,
+    transfer_hbm,
     density,
     out,
     brick,
@@ -51,7 +51,6 @@
     y_send,
     y_recv,
     slots,
-    keep1,
     send1,
     recv1,
     send2,
@@ -60,6 +59,9 @@
     left_of,
     right_of,
     slot_of,
+    occ,
+    transfer,
+    small_sem,
     load_sem,
     window_sem,
     z_sems,
@@ -78,6 +80,12 @@
     far = depth_at + 2 * core - 1
     has_far = jnp.logical_and(far >= 0, far < depth_n)
 
+    small = [
+        pltpu.make_async_copy(occ_hbm, occ, small_sem.at[0]),
+        pltpu.make_async_copy(transfer_hbm, transfer, small_sem.at[1]),
+    ]
+    for copy in small:
+        copy.start()
     barrier = pltpu.get_barrier_semaphore()
 
     def greet(**where):
@@ -118,6 +126,9 @@
     ]
     for copy in window_loads:
         copy.start()
+
+    for copy in small:
+        copy.wait()
 
     for b in range(blocks):
         flags[pl.ds(b, 1), :] = jnp.full((1, LANES), occ[0, 0, b], jnp.int32).astype(jnp.float32)
@@ -315,17 +326,14 @@
             for ch in range(4):
                 send1[c, q, ch] = slots[ring, ch, theirs]
         copy1(c).start()
-        for q in range(blocks // 2):
+
+    def merge(c, ring):
+        copy1(c).wait_recv()
+
+        def merged(q):
             mine = slot_of[4 * (q // 2) + q % 2 + 2 * core]
-            for ch in range(4):
-                keep1[c, q, ch] = slots[ring, ch, mine]
-
-    def merge(c):
-        copy1(c).wait_recv()
-
-        def merged(q):
             return blend(
-                [keep1[c, q, ch] for ch in range(4)],
+                [slots[ring, ch, mine] for ch in range(4)],
                 [recv1[c, q, ch] for ch in range(4)],
                 core == 0,
             )
@@ -393,7 +401,8 @@
     for copy in loads:
         copy.start()
     march_window(0)
-    march_window(1)
+    for t in range(1, AHEAD):
+        march_window(t)
 
     for copy in loads:
         copy.wait()
@@ -450,9 +459,9 @@
             def one_slot(s, inner):
                 march(brick, later_ring, s * GROUP, later_row)
 
-                @pl.when(s == SLOTS // GROUP - 2)
+                @pl.when(s == SLOTS // GROUP - 1)
                 def _():
-                    merge(c)
+                    merge(c, ring)
 
                 return inner
 
@@ -462,7 +471,7 @@
 
     lax.fori_loop(0, CHUNKS, one_chunk, 0)
     for t in range(CHUNKS - AHEAD, CHUNKS):
-        merge(chunk_at(t))
+        merge(chunk_at(t), t % (AHEAD + 1))
     lax.fori_loop(0, CHUNKS, finish, 0)
 
     for side in range(2):
@@ -505,9 +514,9 @@
             functools.partial(kernel, (cells, rows, blocks, depth_n, rows_n)),
             out_shape=jax.ShapeDtypeStruct((4, rows, columns // depth_n), f32),
             in_specs=[
-                pl.BlockSpec(memory_space=pltpu.SMEM),
-                pl.BlockSpec(memory_space=pltpu.SMEM),
-                pl.BlockSpec(memory_space=pl.ANY),
+                pl.BlockSpec(memory_space=pltpu.HBM),
+                pl.BlockSpec(memory_space=pltpu.HBM),
+                pl.BlockSpec(memory_space=pltpu.HBM),
             ],
             out_specs=pl.BlockSpec(memory_space=pltpu.VMEM),
             scratch_shapes=[
@@ -522,13 +531,15 @@
                 pltpu.VMEM((AHEAD + 1, 4, SLOTS + 1) + tile, f32),
                 pltpu.VMEM((CHUNKS, half, 4) + tile, f32),
                 pltpu.VMEM((CHUNKS, half, 4) + tile, f32),
-                pltpu.VMEM((CHUNKS, half, 4) + tile, f32),
                 pltpu.VMEM((CHUNKS, 4, 2, 4) + tile, f32),
                 pltpu.VMEM((CHUNKS, 4, 2, 4) + tile, f32),
                 pltpu.SMEM((SLOTS,), jnp.int32),
                 pltpu.SMEM((blocks,), jnp.int32),
                 pltpu.SMEM((blocks,), jnp.int32),
                 pltpu.SMEM((blocks,), jnp.int32),
+                pltpu.SMEM((1, 1, blocks), jnp.int32),
+                pltpu.SMEM((2, 4), f32),
+                dma((2,)),
                 dma((blocks,)),
                 dma((blocks,)),
                 dma((2, 2, CHUNKS)),
@@ -540,7 +551,7 @@
             compiler_params=pltpu.CompilerParams(
                 collective_id=0,
                 has_side_effects=True,
-                vmem_limit_bytes=60 * 2**20,
+                vmem_limit_bytes=44 * 2**20,
             ),
         )(occupancy, transfer, density)
 

time: 45.8 us -> 44.4 us (0.969)
  Pallas kernels: 43.2 us -> 41.9 us
    pallas_call x1, Pallas kernels: 43.2 us -> 41.9 us  [shards(): pl.pallas_call(functools.partial(kernel, (cells, rows, blocks, depth_n, r...]
    unnamed x1 -> x5, local copies, waits for them, and re-layouts: 1.87 us -> 2.13 us
where the time goes in v4:
time: 44.4 us; the launch traced here: 44 us
  Pallas kernels  41.9 us (94%)
  local copies, waits for them, and re-layouts  2.13 us (5%)
    pallas_call x1, Pallas kernels, shards(): pl.pallas_call(functools.partial(kernel, (cells, rows, blocks, depth_n, r...  41.9 us
    unnamed x5, local copies, waits for them, and re-layouts  2.13 us

profile of v4, /device:TPU:24, one launch (start us, length us, event | category | flops | bytes accessed | tf_op | source)
XLA Modules:
  0.0 44.0 jit_solution(6324709528909384399)
XLA Ops:
  0.0 0.0 copy-start
  0.0 0.7 %copy-done = f32[2,4]{1,0:T(2,128)S(1)} copy-done((f32[2,4]{1,0:T(2,128)S(1)}, f32[2,4]{1,0:T(2,128)}, u32[]{:S(2)}) %copy-start) | copy-done | bytes 56
  0.7 0.0 copy-start.1
  0.7 0.7 %copy-done.1 = s32[1,1,16]{2,1,0:T(1,128)S(1)} copy-done((s32[1,1,16]{2,1,0:T(1,128)S(1)}, s32[1,1,16]{2,1,0:T(1,128)}, u32[]{:S(2)}) %copy-start.1) | copy-done | bytes 88
  1.3 41.9 %shard_map.37 = f32[4,128,256]{2,1,0:T(8,128)S(1)} custom-call(s32[1,1,16]{2,1,0:T(1,128)S(1)} %copy-done.1, f32[2,4]{1,0:T(2,128)S(1)} %copy-done, f32[16,128,2048]{2,1,0:T(8,128)} %density.1), custom_call_target="tpu_custom_call" | custom-call | tf_op jit(solution)/shard_map/pallas_call | solution.py:513
  43.2 0.8 %copy.5 = f32[4,128,256]{2,1,0:T(8,128)} copy(f32[4,128,256]{2,1,0:T(8,128)S(1)} %shard_map.37) | data formatting | bytes 1048576
Async XLA Ops:
  0.0 0.7 %copy-start = (f32[2,4]{1,0:T(2,128)S(1)}, f32[2,4]{1,0:T(2,128)}, u32[]{:S(2)}) copy-start(f32[2,4]{1,0:T(2,128)} %transfer_hbm.1) | copy-start | bytes 100
  0.7 0.7 %copy-start.1 = (s32[1,1,16]{2,1,0:T(1,128)S(1)}, s32[1,1,16]{2,1,0:T(1,128)}, u32[]{:S(2)}) copy-start(s32[1,1,16]{2,1,0:T(1,128)} %occ_hbm.1) | copy-start | bytes 196
